TPU v7x, 32 devices: a whole 2x2x4 slice. The times are simulated.
32 devices in a mesh: rad: 8 (over z, x), azi: 2 (over y), ax: 2 (over core).
Axes of the slice: x: 2, y: 2, z: 4, core: 2. Of those that a mesh axis runs over, the one named last changes fastest.
Arguments:
- density: float32 [512, 16, 1024], P('rad', 'ax', 'azi'), may hold values from 0.5 to 2
- momentum: float32 [3, 512, 16, 1024], P(None, 'rad', 'ax', 'azi'), may hold values from -3 to 3
- energy: float32 [512, 16, 1024], P('rad', 'ax', 'azi'), may hold values from 2 to 4
- register: float32 [5, 512, 16, 1024], P(None, 'rad', 'ax', 'azi'), may hold values from -4 to 4
Outputs:
- register_new: float32 [5, 512, 16, 1024], P(None, 'rad', 'ax', 'azi')
- state_new: float32 [5, 512, 16, 1024], P(None, 'rad', 'ax', 'azi')
All inputs are finite; a program needn't handle non-finite values.
Results may differ from a plain program's by a relative error of at most 0.00012.
Values sent between devices are 32-bit elements; how exact they have to be, the bound alone decides.
A program may use at most 128 MiB of HBM per device.

v0:
```python
import math

import jax
import jax.numpy as jnp
from jax import lax
from jax.sharding import PartitionSpec as P

HEAT_RATIO = 1.4
COURANT = 0.5
SECTION_DECAY = -5.0 / 9.0
SECTION_GAIN = 15.0 / 16.0
CUTOFF_BASE = 4.0
STENCIL = (0.8, -0.2, 4.0 / 105.0, -1.0 / 280.0)


def padded_2(block, sides, width):
    for axis, dim in sides:
        count = lax.axis_size(axis)
        forward = [(i, i + 1) for i in range(count - 1)]
        backward = [(target, source) for source, target in forward]
        low = lax.ppermute(
            lax.slice_in_dim(block, block.shape[dim] - width, None, axis=dim), axis, forward
        )
        high = lax.ppermute(lax.slice_in_dim(block, 0, width, axis=dim), axis, backward)
        block = jnp.concatenate([low, block, high], axis=dim)
    return block


def component(field_id, momentum, velocity, pressure, energy, direction):
    if field_id == 0:
        return momentum[direction]
    if field_id == 4:
        return (energy + pressure) * velocity[direction]
    flux_value = momentum[field_id - 1] * velocity[direction]
    if field_id - 1 == direction:
        flux_value = flux_value + pressure
    return flux_value


def euler_fluxes(density, momentum, energy, directions):
    velocity = momentum / density
    pressure = (HEAT_RATIO - 1.0) * (energy - 0.5 * jnp.sum(momentum * velocity, axis=0))
    return tuple(
        (
            jnp.stack(
                [
                    component(field_id, momentum, velocity, pressure, energy, direction)
                    for field_id in range(5)
                ]
            )
            for direction in directions
        )
    )


def central(padded, length, axis_id, spacing):
    summed = 0.0
    for offset, weight in enumerate(STENCIL, start=1):
        upper_rows = lax.slice_in_dim(padded, 4 + offset, 4 + offset + length, axis=axis_id)
        lower_rows = lax.slice_in_dim(padded, 4 - offset, 4 - offset + length, axis=axis_id)
        summed = summed + weight * (upper_rows - lower_rows)
    return summed / spacing


def flip_rows(values):
    return jnp.flip(values, 1)


def keep_rows(values):
    return values


def per_device(density, momentum, energy, register):
    slabs = lax.axis_size("rad")
    blocks = lax.axis_size("azi")
    rad_index = lax.axis_index("rad")
    azi_index = lax.axis_index("azi")
    row_count, plane_count, angles = density.shape
    radial_total = row_count * slabs
    circle_half = angles * blocks
    spacing = 2.0 / radial_total
    row_ids = rad_index * row_count + jnp.arange(row_count, dtype=jnp.int32)
    radius_col = (-1.0 + (row_ids.astype(jnp.float32) + 0.5) * spacing)[:, None, None]
    column_ids = azi_index * angles + jnp.arange(angles, dtype=jnp.int32)
    azimuths = jnp.pi * column_ids.astype(jnp.float32) / circle_half
    cosine = jnp.cos(azimuths)
    sine_col = jnp.sin(azimuths)
    conserved = jnp.concatenate([density[None], momentum, energy[None]], axis=0)
    flux_x, flux_y, flux_z = euler_fluxes(density, momentum, energy, (0, 1, 2))
    radial_flux = radius_col * (cosine * flux_x + sine_col * flux_y)
    radial_padded = padded_2(radial_flux, (("rad", 1),), 4)
    axial_padded = padded_2(flux_z, (("ax", 2),), 4)
    radial_term = central(radial_padded, row_count, 1, spacing) / radius_col
    axial_term = central(axial_padded, plane_count, 2, spacing)
    mode_ids = jnp.arange(1, circle_half + 1, dtype=jnp.int32)
    point_ids = jnp.arange(circle_half, dtype=jnp.int32)
    turn_ids = point_ids[:, None] * mode_ids[None, :] % (2 * circle_half)
    phases = turn_ids.astype(jnp.float32) * (math.pi / circle_half)
    trig_table = jnp.concatenate([jnp.cos(phases), jnp.sin(phases)], axis=1)
    forward_table = trig_table.reshape(blocks, angles, 2 * circle_half)
    inverse_table = trig_table.T.reshape(2 * circle_half, blocks, angles)
    signs_mode = jnp.where(mode_ids % 2 == 0, 1.0, -1.0).astype(jnp.float32)
    parity = jnp.concatenate([signs_mode, signs_mode])
    mode_float = mode_ids.astype(jnp.float32)
    active = jnp.where(mode_ids < circle_half, mode_float, 0.0)
    group_index = rad_index * blocks + azi_index
    halfway = slabs // 2
    azimuth_flux = jnp.sign(radius_col) * (cosine * flux_y - sine_col * flux_x)
    upper_half = rad_index >= halfway
    ordered = lax.cond(upper_half, flip_rows, keep_rows, azimuth_flux)
    line_total = row_count * plane_count
    received = lax.all_to_all(
        ordered.reshape(5, 1, line_total, angles),
        ("rad", "azi"),
        split_axis=2,
        concat_axis=1,
        tiled=True,
    )
    item_count = received.shape[0]
    line_count = received.shape[2]
    line_ids = group_index * line_count + jnp.arange(line_count, dtype=jnp.int32)
    row_in_slab = line_ids // plane_count
    slab_ids = jnp.arange(slabs, dtype=jnp.int32)
    local_rows = jnp.where(
        slab_ids[None, :] >= halfway, row_count - 1 - row_in_slab[:, None], row_in_slab[:, None]
    )
    global_rows = slab_ids[None, :] * row_count + local_rows
    gathered = received.reshape(item_count, slabs, blocks, line_count, angles)
    distance = jnp.abs(-1.0 + (global_rows.astype(jnp.float32) + 0.5) * spacing)
    slab_count = gathered.shape[1]
    middle = slab_count // 2
    coefficients = jnp.einsum(
        "fsbla,bak->fslk",
        gathered,
        forward_table,
        precision=lax.Precision.HIGHEST,
        preferred_element_type=jnp.float32,
    )
    paired = coefficients[:, middle:] + parity * jnp.flip(coefficients[:, :middle], 1)
    cutoff = CUTOFF_BASE + circle_half * distance.T[middle:, :, None]
    filtered = active / circle_half / (1.0 + (mode_float / cutoff) ** 8)
    rotated = jnp.concatenate(
        [filtered * paired[..., circle_half:], -filtered * paired[..., :circle_half]], axis=-1
    )
    stacked = jnp.concatenate([jnp.flip(parity * rotated, 1), rotated], axis=1)
    result = jnp.einsum(
        "fslk,kba->fsbla",
        stacked,
        inverse_table,
        precision=lax.Precision.HIGHEST,
        preferred_element_type=jnp.float32,
    )
    pieces = result / distance.T[:, None, :, None]
    returned = lax.all_to_all(
        pieces.reshape(item_count, slabs * blocks, line_count, angles),
        ("rad", "azi"),
        split_axis=1,
        concat_axis=2,
        tiled=True,
    )
    azimuthal_term = lax.cond(
        upper_half, flip_rows, keep_rows, returned.reshape(5, row_count, plane_count, angles)
    )
    change = -(radial_term + azimuthal_term + axial_term)
    register_new = SECTION_DECAY * register + COURANT * spacing * change
    state_new = conserved + SECTION_GAIN * register_new
    return (register_new, state_new)


def solution(mesh):
    placed = (
        P("rad", "ax", "azi"),
        P(None, "rad", "ax", "azi"),
        P("rad", "ax", "azi"),
        P(None, "rad", "ax", "azi"),
    )
    return jax.shard_map(
        per_device,
        mesh=mesh,
        in_specs=placed,
        out_specs=(P(None, "rad", "ax", "azi"), P(None, "rad", "ax", "azi")),
        check_vma=False,
    )
```

profile of v0, /device:TPU:20, one launch (start us, length us, event | category | flops | bytes accessed | tf_op | source)
XLA Modules:
  0.0 470.4 jit_solution(9641581094073820598)
XLA Ops:
  0.7 0.0 copy-start
  0.7 2.5 slice_dynamic-update-slice_fusion
  3.1 2.9 multiply_reduce_fusion
  6.0 0.0 copy-start.7
  6.1 0.0 copy-start.1
  6.1 0.0 copy-done
  6.1 0.0 copy-start.5
  6.1 1.3 slice_dynamic-update-slice_fusion.1
  7.4 1.8 multiply_dynamic-update-slice_fusion.3
  9.2 2.3 bitcast_dynamic-update-slice_fusion.3
  11.6 2.4 copy-done.9
  13.9 0.0 copy-done.1
  13.9 1.2 multiply_dynamic-update-slice_fusion.5
  15.2 0.0 copy-start.2
  15.2 0.0 copy-start.6
  15.2 3.4 multiply_dynamic-update-slice_fusion.2
  18.6 2.1 bitcast_dynamic-update-slice_fusion.2
  20.6 7.5 %add_multiply_fusion = (f32[5,64,8,512]{3,2,1,0:T(8,128)}, f32[5,64,8,512]{3,2,1,0:T(8,128)}) fusion(f32[5,64,8,512]{3,2,1,0:T(8,128)} %get-tuple-element.31, f32[5,64,8,512]{3,2,1,0:T(8,128)} %get-tuple-element.32, f32[512]{0:T(512)S(1)} %get-tuple-element.49, f32[512]{0:T(512)S(1)} %get-tuple-element.50, f32[64]{0:T(128)S(1)} %multiply_add_fusion.3, ...), kind=kLoop, calls=%fused_computation.88 | loop fusion | flops 10485760 | bytes 20976128 | tf_op jit(solution)/shard_map/mul | solution.py:90
  28.1 11.4 %conditional.2 = (f32[5,64,8,512]{3,2,1,0:T(8,128)}) conditional(s32[]{:T(128)} %convert_element_type.58, f32[5,64,8,512]{3,2,1,0:T(8,128)} %get-tuple-element.19, f32[5,64,8,512]{3,2,1,0:T(8,128)} %get-tuple-element.19), branch_computations={%region_1.2_spmd, %region_2.3_spmd} | conditional | bytes 20971528 | solution.py:110
  28.1 5.8 %copy.96 = f32[5,64,8,512]{3,2,1,0:T(8,128)} copy(f32[5,64,8,512]{3,2,1,0:T(8,128)} %param.1) | data formatting | bytes 10485760 | tf_op jit(solution)/shard_map/cond
  33.9 5.4 %rev.10 = f32[5,64,8,512]{3,2,1,0:T(8,128)} reverse(f32[5,64,8,512]{3,2,1,0:T(8,128)} %copy.96), dimensions={1} | reverse | bytes 10485760 | tf_op jit(solution)/shard_map/cond/branch_1_fun/jit(_flip)/rev | solution.py:66
  39.5 10.2 %copy.63 = f32[5,1,512,512]{3,1,0,2:T(1,128)} copy(f32[5,1,512,512]{3,2,0,1:T(8,128)} %bitcast.77) | data formatting | bytes 10485760 | tf_op jit(solution)/shard_map/reshape | solution.py:113
  49.7 7.4 %all-to-all-start = ((f32[5,1,512,512]{3,1,0,2:T(1,128)}), f32[5,1,512,512]{3,1,0,2:T(1,128)}, u32[]{:S(2)}, u32[]{:S(2)}) async-start(f32[5,1,512,512]{3,1,0,2:T(1,128)} %copy.63), calls=%async_computation | async-start | bytes 10485760 | tf_op jit(solution)/shard_map/all_to_all | solution.py:112
  57.3 0.1 add_abs_fusion
  57.3 1.3 fusion.67
  58.6 16.4 %fusion.60 = (f32[1024,1024]{1,0:T(8,128)S(1)}, f32[1024,1024]{1,0:T(8,128)S(1)}) fusion(s32[1024]{0:T(1024)S(1)} %iota_add_fusion), kind=kLoop, calls=%fused_computation.105 | loop fusion | flops 14680064 | bytes 8392704 | tf_op jit(solution)/shard_map/cos | solution.py:99
  75.0 3.9 pad_maximum_fusion
  78.8 18.7 %fusion.58 = (f32[2,512,1024]{2,1,0:T(8,128)}, f32[2,512,1024]{2,1,0:T(8,128)}) fusion(s32[1024]{0:T(1024)S(1)} %iota_add_fusion, s32[2,512]{1,0:T(2,128)S(1)} %multiply_add_fusion.1), kind=kLoop, calls=%fused_computation.103 | loop fusion | flops 14680064 | bytes 8396800 | tf_op jit(solution)/shard_map/cos | solution.py:99
  97.5 82.5 %all-to-all-done = f32[5,1,512,512]{3,1,0,2:T(1,128)} async-done(((f32[5,1,512,512]{3,1,0,2:T(1,128)}), f32[5,1,512,512]{3,1,0,2:T(1,128)}, u32[]{:S(2)}, u32[]{:S(2)}) %all-to-all-start) | async-done | bytes 5242912 | tf_op jit(solution)/shard_map/all_to_all | solution.py:112
  180.0 3.5 copy.64
  183.5 0.2 copy-done.10
  183.8 1.3 copy-done.11
  185.0 34.7 %fusion.47 = f32[5,8,32,2048]{3,2,1,0:T(8,128)S(1)} fusion(f32[5,8,2,32,512]{4,3,2,1,0:T(8,128)S(1)} %bitcast.83, f32[2,512,1024]{2,1,0:T(8,128)S(1)} %copy-done.11, f32[2,512,1024]{2,1,0:T(8,128)S(1)} %copy-done.10), kind=kOutput, calls=%fused_computation.89 | convolution fusion | flops 32214351872 | bytes 24117248 | tf_op jit(solution)/shard_map/fsbla,bak->fslk/dot_general | solution.py:132
  219.8 0.6 slice.175
  220.4 1.6 slice_add_fusion
  222.1 0.9 slice_multiply_fusion.1
  223.1 1.5 copy-done.3
  224.6 0.8 copy-done.4
  225.4 2.9 maximum_multiply_fusion
  228.3 5.5 %rev.15 = f32[5,4,32,2048]{3,2,1,0:T(8,128)} reverse(f32[5,4,32,2048]{3,2,1,0:T(8,128)} %maximum_multiply_fusion), dimensions={1} | reverse | bytes 10485760 | tf_op jit(solution)/shard_map/jit(_flip)/rev | solution.py:145
  233.8 40.6 %divide_bitcast_fusion = f32[5,8,2,32,512]{4,3,1,0,2:T(8,128)S(1)} fusion(f32[8,32]{1,0:T(8,128)S(1)} %add_abs_fusion, f32[2048,2,512,1,1]{0,2,4,3,1:T(8,128)} %bitcast.82, f32[5,4,32,1024]{3,2,1,0:T(8,128)} %copy-done.4, f32[5,4,32,1024]{3,2,1,0:T(8,128)} %copy-done.3, f32[5,4,32,2048]{3,2,1,0:T(8,128)} %rev.15), kind=kOutput, calls=%fused_computation.86 | convolution fusion | flops 32218808320 | bytes 24118272 | tf_op jit(solution)/shard_map/fslk,kba->fsbla/dot_general | solution.py:146
  274.4 1.0 copy.66
  275.4 2.9 copy.67
  278.4 7.0 %all-to-all-start.1 = ((f32[5,16,32,512]{3,2,0,1:T(8,128)}), f32[5,16,32,512]{3,2,0,1:T(8,128)}, u32[]{:S(2)}, u32[]{:S(2)}) async-start(f32[5,16,32,512]{3,2,0,1:T(8,128)} %copy.67), calls=%async_computation.1 | async-start | bytes 10485760 | tf_op jit(solution)/shard_map/all_to_all | solution.py:154
  285.4 5.4 %fusion.83 = (f32[5,64,4,512]{3,2,1,0:T(4,128)S(1)}, f32[5,64,4,512]{3,2,1,0:T(4,128)S(1)}) fusion(f32[5,64,8,512]{3,2,1,0:T(8,128)} %get-tuple-element.33), kind=kLoop, calls=%fused_computation.170 | loop fusion | bytes 10485760 | tf_op jit(solution)/shard_map/slice | solution.py:24
  290.8 0.8 copy.69
  291.6 1.3 collective-permute-start.2
  292.9 0.8 copy.71
  293.8 3.4 collective-permute-start.3
  297.1 2.0 fusion.82
  299.1 3.4 collective-permute-start
  302.5 2.5 collective-permute-start.1
  305.0 0.0 collective-permute-done.2
  305.0 3.2 copy.70
  308.1 0.0 collective-permute-done.3
  308.1 3.2 copy.72
  311.3 98.2 %all-to-all-done.1 = f32[5,16,32,512]{3,2,0,1:T(8,128)} async-done(((f32[5,16,32,512]{3,2,0,1:T(8,128)}), f32[5,16,32,512]{3,2,0,1:T(8,128)}, u32[]{:S(2)}, u32[]{:S(2)}) %all-to-all-start.1) | async-done | bytes 5242912 | tf_op jit(solution)/shard_map/all_to_all | solution.py:154
  409.5 5.9 %copy.68 = f32[5,16,32,512]{3,2,1,0:T(8,128)} copy(f32[5,16,32,512]{3,2,0,1:T(8,128)} %all-to-all-done.1) | data formatting | bytes 10485760 | tf_op jit(solution)/shard_map/all_to_all | solution.py:154
  415.5 11.2 %conditional.3 = (f32[5,64,8,512]{3,2,1,0:T(8,128)}) conditional(s32[]{:T(128)} %convert_element_type.58, f32[5,64,8,512]{3,2,1,0:T(8,128)} %bitcast.78, f32[5,64,8,512]{3,2,1,0:T(8,128)} %bitcast.79), branch_computations={%region_3.4_spmd, %region_4.5_spmd} | conditional | bytes 20971528 | solution.py:161
  415.5 5.8 %copy.97 = f32[5,64,8,512]{3,2,1,0:T(8,128)} copy(f32[5,64,8,512]{3,2,1,0:T(8,128)} %param.3) | data formatting | bytes 10485760 | tf_op jit(solution)/shard_map/cond
  421.3 5.4 %rev.11 = f32[5,64,8,512]{3,2,1,0:T(8,128)} reverse(f32[5,64,8,512]{3,2,1,0:T(8,128)} %copy.97), dimensions={1} | reverse | bytes 10485760 | tf_op jit(solution)/shard_map/cond/branch_1_fun/jit(_flip)/rev | solution.py:66
  426.7 0.0 collective-permute-done
  426.7 0.0 collective-permute-done.1
  426.7 43.5 %maximum_add_fusion = (f32[5,64,8,512]{3,2,1,0:T(8,128)}, f32[5,64,8,512]{3,2,1,0:T(8,128)}) fusion(f32[1,64,8,512]{3,2,1,0:T(8,128)} %bitcast.81, f32[3,64,8,512]{3,2,1,0:T(8,128)S(1)} %copy-done, f32[1,64,8,512]{3,2,1,0:T(8,128)} %bitcast.84, f32[5,64,8,512]{3,2,1,0:T(8,128)} %get-tuple-element.33, f32[5,64,4,512]{3,2,1,0:T(4,128)} %copy.72, ...), kind=kLoop, calls=%fused_computation.84 | loop fusion | flops 66846720 | bytes 42598656 | tf_op jit(solution)/shard_map/add | solution.py:166
  (28 shorter events, 0.2 us)
Async XLA Ops:
  0.7 5.4 %copy-start = (f32[3,64,8,512]{3,2,1,0:T(8,128)S(1)}, f32[3,64,8,512]{3,2,1,0:T(8,128)}, u32[]{:S(2)}) copy-start(f32[3,64,8,512]{3,2,1,0:T(8,128)} %param.9) | copy-start | bytes 9437188
  6.0 3.2 copy-start.7
  6.1 7.9 %copy-start.1 = (f32[3,64,8,512]{3,2,1,0:T(8,128)}, f32[3,64,8,512]{3,2,1,0:T(8,128)S(1)}, u32[]{:S(2)}) copy-start(f32[3,64,8,512]{3,2,1,0:T(8,128)S(1)} %get-tuple-element.37) | copy-start | bytes 9437188
  6.1 3.2 copy-start.5
  11.6 2.4 copy-start.9
  15.2 3.4 copy-start.2
  15.2 3.4 copy-start.6
  15.2 3.4 copy-start.8
  49.7 130.3 %all-to-all-start = ((f32[5,1,512,512]{3,1,0,2:T(1,128)}), f32[5,1,512,512]{3,1,0,2:T(1,128)}, u32[]{:S(2)}, u32[]{:S(2)}) async-start(f32[5,1,512,512]{3,1,0,2:T(1,128)} %copy.63), calls=%async_computation | async-start | bytes 10485760 | tf_op jit(solution)/shard_map/all_to_all | solution.py:112
  180.0 3.7 copy-start.10
  180.0 5.0 %copy-start.11 = (f32[2,512,1024]{2,1,0:T(8,128)S(1)}, f32[2,512,1024]{2,1,0:T(8,128)}, u32[]{:S(2)}) copy-start(f32[2,512,1024]{2,1,0:T(8,128)} %get-tuple-element.44) | copy-start | bytes 12582916
  220.4 1.7 copy-start.12
  220.4 1.7 copy-start.13
  223.0 1.5 copy-start.3
  223.1 2.3 copy-start.4
  278.4 131.2 %all-to-all-start.1 = ((f32[5,16,32,512]{3,2,0,1:T(8,128)}), f32[5,16,32,512]{3,2,0,1:T(8,128)}, u32[]{:S(2)}, u32[]{:S(2)}) async-start(f32[5,16,32,512]{3,2,0,1:T(8,128)} %copy.67), calls=%async_computation.1 | async-start | bytes 10485760 | tf_op jit(solution)/shard_map/all_to_all | solution.py:154
  291.6 13.3 %collective-permute-start.2 = (f32[5,64,4,512]{3,1,2,0:T(8,128)S(1)}, f32[5,64,4,512]{3,1,2,0:T(8,128)S(1)}, u32[]{:S(2)}, u32[]{:S(2)}) collective-permute-start(f32[5,64,4,512]{3,1,2,0:T(8,128)S(1)} %copy.69), channel_id=1, source_target_pairs={{1,0},{3,2},{5,4},{7,6},{9,8},{11,10},{13,12},{15,14},{17,16},{19,... | collective-permute-start | bytes 7864328 | tf_op jit(solution)/shard_map/ppermute | solution.py:24
  293.8 14.4 %collective-permute-start.3 = (f32[5,64,4,512]{3,1,2,0:T(8,128)S(1)}, f32[5,64,4,512]{3,1,2,0:T(8,128)S(1)}, u32[]{:S(2)}, u32[]{:S(2)}) collective-permute-start(f32[5,64,4,512]{3,1,2,0:T(8,128)S(1)} %copy.71), channel_id=1, source_target_pairs={{0,1},{2,3},{4,5},{6,7},{8,9},{10,11},{12,13},{14,15},{16,17},{18,... | collective-permute-start | bytes 7864328 | tf_op jit(solution)/shard_map/ppermute | solution.py:21
  299.1 127.6 %collective-permute-start = (f32[5,4,8,512]{3,2,1,0:T(8,128)}, f32[5,4,8,512]{3,2,1,0:T(8,128)S(1)}, u32[]{:S(2)}, u32[]{:S(2)}) collective-permute-start(f32[5,4,8,512]{3,2,1,0:T(8,128)} %get-tuple-element.27), channel_id=1, source_target_pairs={{4,0},{8,4},{12,8},{16,12},{20,16},{24,20},{28,24},{5,1},{9,5},{13... | collective-permute-start | bytes 983048 | tf_op jit(solution)/shard_map/ppermute | solution.py:24
  302.5 124.2 %collective-permute-start.1 = (f32[5,4,8,512]{3,2,1,0:T(8,128)}, f32[5,4,8,512]{3,2,1,0:T(8,128)}, u32[]{:S(2)}, u32[]{:S(2)}) collective-permute-start(f32[5,4,8,512]{3,2,1,0:T(8,128)} %get-tuple-element.28), channel_id=1, source_target_pairs={{0,4},{4,8},{8,12},{12,16},{16,20},{20,24},{24,28},{1,5},{5,9},{9,... | collective-permute-start | bytes 983048 | tf_op jit(solution)/shard_map/ppermute | solution.py:21
where the time goes:
time: 476 us; the launch traced here: 470 us
  waiting for transfers between devices  181 us (38%)
  other arithmetic  112 us (24%)
  local copies, waits for them, and re-layouts  76.3 us (16%)
  matrix products  75.3 us (16%)
  starting transfers between devices  24.9 us (5%)
    all_to_all x1, waiting for transfers between devices, per_device(): lax.all_to_all(pieces.reshape(item_count, slabs * blocks, line_count, ang...  98.2 us
    all_to_all x1, waiting for transfers between devices, per_device(): lax.all_to_all(ordered.reshape(5, 1, line_total, angles), ('rad', 'azi'),...  82.5 us
    add x1, other arithmetic, per_device(): state_new = conserved + SECTION_GAIN * register_new  43.5 us
    dot_general x1, matrix products, per_device(): jnp.einsum('fslk,kba->fsbla', stacked, inverse_table, precision=lax.Preci...  40.6 us
    cos x2, other arithmetic, per_device(): trig_table = jnp.concatenate([jnp.cos(phases), jnp.sin(phases)], axis=1)  35 us
    dot_general x1, matrix products, per_device(): jnp.einsum('fsbla,bak->fslk', gathered, forward_table, precision=lax.Prec...  34.7 us
    cond x2, local copies, waits for them, and re-layouts  11.6 us
    rev x2, local copies, waits for them, and re-layouts, flip_rows(): return jnp.flip(values, 1)  10.8 us
  transfers between devices with their start and end apart: 6, of which 2 were waited for; matrix products, arithmetic and copies ran while one was open for 15% of the time, Pallas kernels for 0%

commit v1 on v0

v1 whole, which is shorter than its diff:
```python
import numpy as np
import jax
import jax.numpy as jnp
from jax import lax
from jax.sharding import PartitionSpec as P

HEAT_RATIO = 1.4
COURANT = 0.5
SECTION_DECAY = -5.0 / 9.0
SECTION_GAIN = 15.0 / 16.0
CUTOFF_BASE = 4.0
STENCIL = (0.8, -0.2, 4.0 / 105.0, -1.0 / 280.0)
CUTS = 1
DEPTH = 2


def trig_tables(half):
    points = np.arange(half)[:, None]
    tables = []
    for modes in (np.arange(0, half, 2), np.arange(1, half, 2)):
        phases = (points * modes[None, :] % (2 * half)) * (np.pi / half)
        tables.append(np.concatenate([np.cos(phases), np.sin(phases)], axis=1).astype(np.float32))
    return tables


def padded_2(block, axis, dim, width):
    count = lax.axis_size(axis)
    forward = [(i, i + 1) for i in range(count - 1)]
    backward = [(target, source) for source, target in forward]
    low = lax.ppermute(lax.slice_in_dim(block, block.shape[dim] - width, None, axis=dim), axis, forward)
    high = lax.ppermute(lax.slice_in_dim(block, 0, width, axis=dim), axis, backward)
    return low, high


def central(padded, length, axis_id, spacing):
    summed = 0.0
    for offset, weight in enumerate(STENCIL, start=1):
        upper_rows = lax.slice_in_dim(padded, 4 + offset, 4 + offset + length, axis=axis_id)
        lower_rows = lax.slice_in_dim(padded, 4 - offset, 4 - offset + length, axis=axis_id)
        summed = summed + weight * (upper_rows - lower_rows)
    return summed / spacing


def component(field_id, momentum, velocity, pressure, energy, direction):
    if field_id == 0:
        return momentum[direction]
    if field_id == 4:
        return (energy + pressure) * velocity[direction]
    flux_value = momentum[field_id - 1] * velocity[direction]
    if field_id - 1 == direction:
        flux_value = flux_value + pressure
    return flux_value


def per_device(density, momentum, energy, register):
    slabs = lax.axis_size("rad")
    blocks = lax.axis_size("azi")
    rad_index = lax.axis_index("rad")
    azi_index = lax.axis_index("azi")
    row_count, plane_count, angles = density.shape
    radial_total = row_count * slabs
    half = angles * blocks
    spacing = 2.0 / radial_total
    row_ids = rad_index * row_count + jnp.arange(row_count, dtype=jnp.int32)
    radius_col = (-1.0 + (row_ids.astype(jnp.float32) + 0.5) * spacing)[:, None, None]
    column_ids = azi_index * angles + jnp.arange(angles, dtype=jnp.int32)
    azimuths = jnp.pi * column_ids.astype(jnp.float32) / half
    cosine = jnp.cos(azimuths)
    sine_col = jnp.sin(azimuths)
    upper = rad_index >= slabs // 2
    group_rows = row_count // blocks
    cuts = CUTS if group_rows % CUTS == 0 else 1
    piece = group_rows // cuts

    velocity = momentum / density
    pressure = (HEAT_RATIO - 1.0) * (energy - 0.5 * jnp.sum(momentum * velocity, axis=0))
    conserved = [density, momentum[0], momentum[1], momentum[2], energy]

    def flux(field_id, direction):
        return component(field_id, momentum, velocity, pressure, energy, direction)

    sign = jnp.where(upper, 1.0, -1.0).astype(jnp.float32)
    azimuth_flux = [
        (sign * cosine) * flux(f, 1) - (sign * sine_col) * flux(f, 0) for f in range(5)
    ]

    even_table, odd_table = trig_tables(half)
    mode_even = jnp.arange(0, half, 2, dtype=jnp.int32).astype(jnp.float32)
    mode_odd = jnp.arange(1, half, 2, dtype=jnp.int32).astype(jnp.float32)

    def group_of(member):
        return jnp.where(upper, member, blocks - 1 - member)

    mirror = [
        (r * blocks + a, (slabs - 1 - r) * blocks + a) for r in range(slabs) for a in range(blocks)
    ]

    def start_of(member, part):
        inner = jnp.where(upper, part, cuts - 1 - part)
        return group_of(member) * group_rows + inner * piece

    def gather_azi(values, part):
        whole = jnp.zeros((piece, plane_count, half), jnp.float32)
        own = lax.dynamic_slice_in_dim(values, start_of(azi_index, part), piece, 0)
        whole = lax.dynamic_update_slice_in_dim(whole, own, azi_index * angles, 2)
        for shift in range(1, blocks):
            target = (azi_index + shift) % blocks
            source = (azi_index + blocks - shift) % blocks
            sent = lax.dynamic_slice_in_dim(values, start_of(target, part), piece, 0)
            got = lax.ppermute(sent, "azi", [(a, (a + shift) % blocks) for a in range(blocks)])
            whole = lax.dynamic_update_slice_in_dim(whole, got, source * angles, 2)
        return whole

    def derive(own, other, part):
        rows = rad_index * row_count + start_of(azi_index, part) + jnp.arange(piece, dtype=jnp.int32)
        distance = jnp.abs(-1.0 + (rows.astype(jnp.float32) + 0.5) * spacing)[:, None, None]
        cutoff = CUTOFF_BASE + half * distance
        result = 0.0
        for values, table, modes in (
            (own + other, even_table, mode_even),
            (own - other, odd_table, mode_odd),
        ):
            filtered = modes / half / (1.0 + (modes / cutoff) ** 8) / distance
            sums = lax.dot_general(
                values.reshape(piece * plane_count, half), table, (((1,), (0,)), ((), ())),
                precision=lax.Precision.HIGH, preferred_element_type=jnp.float32,
            ).reshape(piece, plane_count, half)
            turned = jnp.concatenate(
                [filtered * sums[..., half // 2 :], -filtered * sums[..., : half // 2]], axis=-1
            )
            result = result + lax.dot_general(
                turned.reshape(piece * plane_count, half), table, (((1,), (1,)), ((), ())),
                precision=lax.Precision.HIGH, preferred_element_type=jnp.float32,
            )
        return result.reshape(piece, plane_count, half)

    def scatter_azi(total, values, part):
        own = lax.dynamic_slice_in_dim(values, azi_index * angles, angles, 2)
        total = lax.dynamic_update_slice_in_dim(total, own, start_of(azi_index, part), 0)
        for shift in range(1, blocks):
            target = (azi_index + shift) % blocks
            source = (azi_index + blocks - shift) % blocks
            sent = lax.dynamic_slice_in_dim(values, target * angles, angles, 2)
            got = lax.ppermute(sent, "azi", [(a, (a + shift) % blocks) for a in range(blocks)])
            total = lax.dynamic_update_slice_in_dim(total, got, start_of(source, part), 0)
        return total

    steps = [(f, part) for f in range(5) for part in range(cuts)]
    azimuthal = [jnp.zeros((row_count, plane_count, angles), jnp.float32) for _ in range(5)]
    arrived = []
    for index, (f, part) in enumerate(steps):
        own = gather_azi(azimuth_flux[f], part)
        if index >= DEPTH:
            own, arrived[index - DEPTH] = lax.optimization_barrier((own, arrived[index - DEPTH]))
        other = lax.ppermute(own, ("rad", "azi"), mirror)
        arrived.append((own, other))
    for index, (f, part) in enumerate(steps):
        own, other = arrived[index]
        derived = derive(own, jnp.flip(other, 0), part)
        azimuthal[f] = scatter_azi(azimuthal[f], derived, part)

    flux_x, flux_y, flux_z = (jnp.stack([flux(f, c) for f in range(5)]) for c in range(3))
    radial_flux = radius_col * (cosine * flux_x + sine_col * flux_y)
    low, high = padded_2(radial_flux, "rad", 1, 4)
    radial_padded = jnp.concatenate([low, radial_flux, high], axis=1)
    low, high = padded_2(flux_z, "ax", 2, 4)
    axial_padded = jnp.concatenate([low, flux_z, high], axis=2)
    radial_term = central(radial_padded, row_count, 1, spacing) / radius_col
    axial_term = central(axial_padded, plane_count, 2, spacing)
    base = SECTION_DECAY * register - COURANT * spacing * (radial_term + axial_term)
    base = lax.optimization_barrier(base)
    register_new = jnp.stack([base[f] - COURANT * spacing * azimuthal[f] for f in range(5)])
    state_new = jnp.stack(conserved) + SECTION_GAIN * register_new
    return (register_new, state_new)


def solution(mesh):
    placed = (
        P("rad", "ax", "azi"),
        P(None, "rad", "ax", "azi"),
        P("rad", "ax", "azi"),
        P(None, "rad", "ax", "azi"),
    )
    return jax.shard_map(
        per_device,
        mesh=mesh,
        in_specs=placed,
        out_specs=(P(None, "rad", "ax", "azi"), P(None, "rad", "ax", "azi")),
        check_vma=False,
    )
```

time: 476 us -> 428 us (0.90)
  the two profiles are of different devices: /device:TPU:20 before, /device:TPU:8 now
where the time goes in v1:
time: 428 us; the launch traced here: 420 us
  waiting for transfers between devices  200 us (47%)
  other arithmetic  89.7 us (21%)
  matrix products  62.8 us (15%)
  local copies, waits for them, and re-layouts  34.4 us (8%)
  starting transfers between devices  31.2 us (7%)
    ppermute x5, waiting for transfers between devices, per_device(): other = lax.ppermute(own, ('rad', 'azi'), mirror)  143 us
    sub x1, other arithmetic, per_device(): SECTION_DECAY * register - COURANT * spacing * (radial_term + axial_term)  51 us
    dot_general x10, matrix products, derive(): lax.dot_general(values.reshape(piece * plane_count, half), table, (((1,),...  40.8 us
    ppermute x5, waiting for transfers between devices, scatter_azi(): lax.ppermute(sent, 'azi', [(a, (a + shift) % blocks) for a in range(block...  30 us
    ppermute x5, waiting for transfers between devices, gather_azi(): lax.ppermute(sent, 'azi', [(a, (a + shift) % blocks) for a in range(block...  26.8 us
    dot_general x10, matrix products, derive(): lax.dot_general(turned.reshape(piece * plane_count, half), table, (((1,),...  22.1 us
    unnamed x10, other arithmetic  11.3 us
    ppermute x5, starting transfers between devices, per_device(): other = lax.ppermute(own, ('rad', 'azi'), mirror)  9.45 us
  transfers between devices with their start and end apart: 19, of which 10 were waited for; matrix products, arithmetic and copies ran while one was open for 33% of the time, Pallas kernels for 0%

profile of v1, /device:TPU:8, one launch (start us, length us, event | category | flops | bytes accessed | tf_op | source)
XLA Modules:
  0.0 419.8 jit_solution(4128194991002566374)
XLA Ops:
  0.6 2.3 slice_dynamic-update-slice_fusion
  2.9 3.9 multiply_reduce_fusion
  6.8 3.3 slice_dynamic-update-slice_fusion.1
  10.2 1.9 multiply_dynamic-update-slice_fusion.3
  12.1 3.2 multiply_subtract_fusion.1
  15.3 2.3 bitcast_dynamic-update-slice_fusion.5
  18.8 1.7 multiply_dynamic-update-slice_fusion.4
  21.2 1.8 bitcast_dynamic-update-slice_fusion.4
  23.0 3.6 fusion.140
  26.9 3.2 collective-permute-start.3
  30.1 3.0 fusion.89
  33.2 2.3 constant_dynamic-slice_fusion.8
  35.5 1.5 collective-permute-start.4
  37.1 2.1 constant_dynamic-slice_fusion.7
  41.9 1.5 collective-permute-start.12
  45.0 8.1 %add_multiply_fusion = f32[5,64,8,512]{3,2,1,0:T(8,128)} fusion(f32[5,64,8,512]{3,2,1,0:T(8,128)} %get-tuple-element.39, f32[5,64,8,512]{3,2,1,0:T(8,128)} %get-tuple-element.37, f32[512]{0:T(512)S(1)} %get-tuple-element.110, f32[512]{0:T(512)S(1)} %get-tuple-element.111, f32[64]{0:T(128)S(1)} %multiply_add_fusion.1), kind=kLoop, calls=%fused_computation.64 | loop fusion | flops 5242880 | bytes 15732992 | tf_op jit(solution)/shard_map/mul | solution.py:163
  55.3 6.6 %collective-permute-done.5 = f32[32,8,512]{2,1,0:T(8,128)} collective-permute-done((f32[32,8,512]{2,1,0:T(8,128)}, f32[32,8,512]{2,1,0:T(8,128)}, u32[]{:S(2)}, u32[]{:S(2)}) %collective-permute-start.5) | collective-permute-done | bytes 524320 | tf_op jit(solution)/shard_map/ppermute | solution.py:110
  64.3 17.0 %collective-permute-done.9 = f32[32,8,512]{2,1,0:T(8,128)} collective-permute-done((f32[32,8,512]{2,1,0:T(8,128)}, f32[32,8,512]{2,1,0:T(8,128)}, u32[]{:S(2)}, u32[]{:S(2)}) %collective-permute-start.9) | collective-permute-done | bytes 524320 | tf_op jit(solution)/shard_map/ppermute | solution.py:110
  81.2 2.5 collective-permute-start.6
  85.4 1.6 collective-permute-start.8
  87.8 1.9 fusion.139
  90.7 1.9 constant_dynamic-update-slice_fusion
  92.7 3.3 collective-permute-done.8
  95.9 3.4 collective-permute-start.1
  100.2 95.2 %collective-permute-done.6 = f32[32,8,1024]{2,1,0:T(8,128)S(1)} collective-permute-done((f32[32,8,1024]{2,1,0:T(8,128)S(1)}, f32[32,8,1024]{2,1,0:T(8,128)S(1)}, u32[]{:S(2)}, u32[]{:S(2)}) %collective-permute-start.6) | collective-permute-done | bytes 1048608 | tf_op jit(solution)/shard_map/ppermute | solution.py:155
  196.4 2.4 collective-permute-start
  198.8 1.3 rev.16
  200.0 45.1 %collective-permute-done.10 = f32[32,8,1024]{2,1,0:T(8,128)} collective-permute-done((f32[32,8,1024]{2,1,0:T(8,128)S(1)}, f32[32,8,1024]{2,1,0:T(8,128)}, u32[]{:S(2)}, u32[]{:S(2)}) %collective-permute-start.10) | collective-permute-done | bytes 1048608 | tf_op jit(solution)/shard_map/ppermute | solution.py:155
  245.1 3.5 collective-permute-start.13
  248.6 1.3 rev.17
  249.9 5.7 %fusion.112 = f32[32,8,1024]{2,1,0:T(8,128)} fusion(f32[1024,1024,1]{1,0,2:T(8,128)} %constant.136, f32[32,8,1024]{2,1,0:T(8,128)} %copy-done.12, f32[32,8,1024]{2,1,0:T(8,128)S(1)} %rev.16), kind=kOutput, calls=%fused_computation.180 | convolution fusion | flops 1610874880 | bytes 7340032 | tf_op jit(solution)/shard_map/dot_general | solution.py:124
  255.7 3.3 fusion.110
  258.9 3.3 fusion.108
  262.2 3.3 fusion.106
  265.5 51.0 %multiply_subtract_fusion = f32[5,64,8,512]{3,2,1,0:T(8,128)} fusion(f32[5,64,8,512]{3,2,1,0:T(8,128)} %param.9, f32[5,64,8,512]{3,2,1,0:T(8,128)} %copy-done.11, f32[5,64,4,512]{3,2,1,0:T(4,128)} %collective-permute-done.3, f32[5,64,4,512]{3,2,1,0:T(4,128)} %collective-permute-done.2, f32[5,64,8,512]{3,2,1,0:T(8,128)} %add_multiply_fusion, ...), kind=kLoop, calls=%fused_computation.63 | loop fusion | flops 58982400 | bytes 26870016 | tf_op jit(solution)/shard_map/sub | solution.py:170
  316.5 3.0 collective-permute-start.17
  319.6 5.5 %fusion.100 = f32[32,8,1024]{2,1,0:T(8,128)} fusion(f32[1024,1024,1]{1,0,2:T(8,128)} %constant.136, f32[32,8,1024]{2,1,0:T(8,128)} %constant_dynamic-update-slice_fusion.5, f32[32,8,1024]{2,1,0:T(8,128)S(1)} %rev.19), kind=kOutput, calls=%fused_computation.167 | convolution fusion | flops 1610874880 | bytes 7340032 | tf_op jit(solution)/shard_map/dot_general | solution.py:124
  326.4 5.7 %fusion.98 = f32[32,8,1024]{2,1,0:T(8,128)} fusion(f32[1024,1024,1]{1,0,2:T(8,128)} %constant.137, f32[32,8,1024]{2,1,0:T(8,128)} %constant_dynamic-update-slice_fusion.5, f32[32,8,1024]{2,1,0:T(8,128)S(1)} %rev.19), kind=kOutput, calls=%fused_computation.165 | convolution fusion | flops 1610874880 | bytes 7340032 | tf_op jit(solution)/shard_map/dot_general | solution.py:124
  332.2 3.3 fusion.104
  335.4 2.3 fusion.102
  337.7 2.9 collective-permute-done.17
  340.6 1.3 rev.20
  341.9 4.7 %fusion.96 = f32[32,8,1024]{2,1,0:T(8,128)S(1)} fusion(f32[1024,1024,1]{1,0,2:T(8,128)} %constant.136, f32[32,8,1024]{2,1,0:T(8,128)} %constant_dynamic-update-slice_fusion, f32[32,8,1024]{2,1,0:T(8,128)S(1)} %rev.20), kind=kOutput, calls=%fused_computation.163 | convolution fusion | flops 1610874880 | bytes 7340032 | tf_op jit(solution)/shard_map/dot_general | solution.py:124
  346.7 3.7 fusion.94
  350.5 1.3 slice_multiply_fusion.19
  352.7 2.2 fusion.58
  355.8 1.3 copy-done.3
  357.1 2.2 fusion.42
  359.5 1.6 collective-permute-start.7
  361.1 2.2 fusion.63
  363.3 2.2 fusion.41
  366.3 2.2 fusion.68
  368.5 2.4 fusion.40
  371.1 1.6 collective-permute-start.14
  372.6 2.2 fusion.73
  374.8 2.2 fusion.39
  377.8 2.2 fusion.78
  380.0 2.2 fusion.38
  382.5 1.6 collective-permute-start.18
  384.1 1.6 collective-permute-done.11
  385.8 11.2 %collective-permute-done.14 = f32[32,8,512]{2,1,0:T(8,128)S(1)} collective-permute-done((f32[32,8,512]{2,1,0:T(8,128)S(1)}, f32[32,8,512]{2,1,0:T(8,128)S(1)}, u32[]{:S(2)}, u32[]{:S(2)}) %collective-permute-start.14) | collective-permute-done | bytes 524320 | tf_op jit(solution)/shard_map/ppermute | solution.py:144
  397.5 10.7 %collective-permute-done.16 = f32[32,8,512]{2,1,0:T(8,128)S(1)} collective-permute-done((f32[32,8,512]{2,1,0:T(8,128)S(1)}, f32[32,8,512]{2,1,0:T(8,128)S(1)}, u32[]{:S(2)}, u32[]{:S(2)}) %collective-permute-start.16) | collective-permute-done | bytes 524320 | tf_op jit(solution)/shard_map/ppermute | solution.py:144
  408.7 6.5 %collective-permute-done.18 = f32[32,8,512]{2,1,0:T(8,128)S(1)} collective-permute-done((f32[32,8,512]{2,1,0:T(8,128)S(1)}, f32[32,8,512]{2,1,0:T(8,128)S(1)}, u32[]{:S(2)}, u32[]{:S(2)}) %collective-permute-start.18) | collective-permute-done | bytes 524320 | tf_op jit(solution)/shard_map/ppermute | solution.py:144
  415.5 4.0 maximum_add_fusion
  (129 shorter events, 23.3 us)
Async XLA Ops:
  6.8 3.3 copy-start
  12.1 3.2 copy-start.1
  17.6 3.6 copy-start.10
  23.0 3.9 copy-start.11
  26.9 238.6 %collective-permute-start.3 = (f32[5,64,4,512]{3,2,1,0:T(4,128)}, f32[5,64,4,512]{3,2,1,0:T(4,128)}, u32[]{:S(2)}, u32[]{:S(2)}) collective-permute-start(f32[5,64,4,512]{3,2,1,0:T(4,128)} %get-tuple-element.36), channel_id=1, source_target_pairs={{0,1},{2,3},{4,5},{6,7},{8,9},{10,11},{12,13},{14,15},{16,17},{18,... | collective-permute-start | bytes 7864328 | tf_op jit(solution)/shard_map/ppermute | solution.py:30
  33.1 7.7 %copy-start.17 = (f32[64,8,512]{2,1,0:T(8,128)S(1)}, f32[64,8,512]{2,1,0:T(8,128)}, u32[]{:S(2)}) copy-start(f32[64,8,512]{2,1,0:T(8,128)} %get-tuple-element.20) | copy-start | bytes 3145732
  33.1 10.4 %copy-start.19 = (f32[64,8,512]{2,1,0:T(8,128)S(1)}, f32[64,8,512]{2,1,0:T(8,128)}, u32[]{:S(2)}) copy-start(f32[64,8,512]{2,1,0:T(8,128)} %get-tuple-element.23) | copy-start | bytes 3145732
  35.5 49.4 %collective-permute-start.4 = (f32[32,8,512]{2,1,0:T(8,128)}, f32[32,8,512]{2,1,0:T(8,128)}, u32[]{:S(2)}, u32[]{:S(2)}) collective-permute-start(f32[32,8,512]{2,1,0:T(8,128)} %get-tuple-element.84), channel_id=1, source_target_pairs={{0,2},{2,0},{1,3},{3,1},{4,6},{6,4},{5,7},{7,5},{8,10},{10,8},{9,1... | collective-permute-start | bytes 1572872 | tf_op jit(solution)/shard_map/ppermute | solution.py:110
  39.2 22.7 %collective-permute-start.5 = (f32[32,8,512]{2,1,0:T(8,128)}, f32[32,8,512]{2,1,0:T(8,128)}, u32[]{:S(2)}, u32[]{:S(2)}) collective-permute-start(f32[32,8,512]{2,1,0:T(8,128)} %get-tuple-element.82), channel_id=1, source_target_pairs={{0,2},{2,0},{1,3},{3,1},{4,6},{6,4},{5,7},{7,5},{8,10},{10,8},{9,1... | collective-permute-start | bytes 1572872 | tf_op jit(solution)/shard_map/ppermute | solution.py:110
  41.9 43.5 %collective-permute-start.12 = (f32[32,8,512]{2,1,0:T(8,128)}, f32[32,8,512]{2,1,0:T(8,128)}, u32[]{:S(2)}, u32[]{:S(2)}) collective-permute-start(f32[32,8,512]{2,1,0:T(8,128)} %get-tuple-element.64), channel_id=1, source_target_pairs={{0,2},{2,0},{1,3},{3,1},{4,6},{6,4},{5,7},{7,5},{8,10},{10,8},{9,1... | collective-permute-start | bytes 1572872 | tf_op jit(solution)/shard_map/ppermute | solution.py:110
  44.4 36.8 %collective-permute-start.9 = (f32[32,8,512]{2,1,0:T(8,128)}, f32[32,8,512]{2,1,0:T(8,128)}, u32[]{:S(2)}, u32[]{:S(2)}) collective-permute-start(f32[32,8,512]{2,1,0:T(8,128)} %get-tuple-element.72), channel_id=1, source_target_pairs={{0,2},{2,0},{1,3},{3,1},{4,6},{6,4},{5,7},{7,5},{8,10},{10,8},{9,1... | collective-permute-start | bytes 1572872 | tf_op jit(solution)/shard_map/ppermute | solution.py:110
  45.0 9.2 %copy-start.18 = (f32[64,8,512]{2,1,0:T(8,128)S(1)}, f32[64,8,512]{2,1,0:T(8,128)}, u32[]{:S(2)}) copy-start(f32[64,8,512]{2,1,0:T(8,128)} %get-tuple-element.28) | copy-start | bytes 3145732
  61.9 203.6 %collective-permute-start.2 = (f32[5,64,4,512]{3,2,1,0:T(4,128)}, f32[5,64,4,512]{3,2,1,0:T(4,128)}, u32[]{:S(2)}, u32[]{:S(2)}) collective-permute-start(f32[5,64,4,512]{3,2,1,0:T(4,128)} %get-tuple-element.35), channel_id=1, source_target_pairs={{1,0},{3,2},{5,4},{7,6},{9,8},{11,10},{13,12},{15,14},{17,16},{19,... | collective-permute-start | bytes 7864328 | tf_op jit(solution)/shard_map/ppermute | solution.py:31
  64.3 131.1 %copy-start.12 = (f32[32,8,1024]{2,1,0:T(8,128)}, f32[32,8,1024]{2,1,0:T(8,128)S(1)}, u32[]{:S(2)}) copy-start(f32[32,8,1024]{2,1,0:T(8,128)S(1)} %constant_dynamic-update-slice_fusion.7) | copy-start | bytes 3145732
  81.2 114.1 %collective-permute-start.6 = (f32[32,8,1024]{2,1,0:T(8,128)S(1)}, f32[32,8,1024]{2,1,0:T(8,128)S(1)}, u32[]{:S(2)}, u32[]{:S(2)}) collective-permute-start(f32[32,8,1024]{2,1,0:T(8,128)S(1)} %constant_dynamic-update-slice_fusion.7), channel_id=1, source_target_pairs={{0,28},{2,30},{4,24},{6,26},{8,20},{10,22},{12,16},{14,18},{16,12}... | collective-permute-start | bytes 3145736 | tf_op jit(solution)/shard_map/ppermute | solution.py:155
  84.8 160.3 %copy-start.14 = (f32[32,8,1024]{2,1,0:T(8,128)}, f32[32,8,1024]{2,1,0:T(8,128)S(1)}, u32[]{:S(2)}) copy-start(f32[32,8,1024]{2,1,0:T(8,128)S(1)} %constant_dynamic-update-slice_fusion.4) | copy-start | bytes 3145732
  84.9 160.3 %collective-permute-start.10 = (f32[32,8,1024]{2,1,0:T(8,128)S(1)}, f32[32,8,1024]{2,1,0:T(8,128)}, u32[]{:S(2)}, u32[]{:S(2)}) collective-permute-start(f32[32,8,1024]{2,1,0:T(8,128)S(1)} %constant_dynamic-update-slice_fusion.4), channel_id=1, source_target_pairs={{0,28},{2,30},{4,24},{6,26},{8,20},{10,22},{12,16},{14,18},{16,12}... | collective-permute-start | bytes 3145736 | tf_op jit(solution)/shard_map/ppermute | solution.py:155
  85.4 10.5 %collective-permute-start.8 = (f32[32,8,512]{2,1,0:T(8,128)}, f32[32,8,512]{2,1,0:T(8,128)S(1)}, u32[]{:S(2)}, u32[]{:S(2)}) collective-permute-start(f32[32,8,512]{2,1,0:T(8,128)} %get-tuple-element.74), channel_id=1, source_target_pairs={{0,2},{2,0},{1,3},{3,1},{4,6},{6,4},{5,7},{7,5},{8,10},{10,8},{9,1... | collective-permute-start | bytes 1572872 | tf_op jit(solution)/shard_map/ppermute | solution.py:110
  95.9 169.6 %collective-permute-start.1 = (f32[5,4,8,512]{3,2,1,0:T(8,128)}, f32[5,4,8,512]{3,2,1,0:T(8,128)}, u32[]{:S(2)}, u32[]{:S(2)}) collective-permute-start(f32[5,4,8,512]{3,2,1,0:T(8,128)} %get-tuple-element.34), channel_id=1, source_target_pairs={{0,4},{4,8},{8,12},{12,16},{16,20},{20,24},{24,28},{1,5},{5,9},{9,... | collective-permute-start | bytes 983048 | tf_op jit(solution)/shard_map/ppermute | solution.py:30
  195.4 1.0 copy-start.29
  196.4 69.1 %collective-permute-start = (f32[5,4,8,512]{3,2,1,0:T(8,128)S(1)}, f32[5,4,8,512]{3,2,1,0:T(8,128)}, u32[]{:S(2)}, u32[]{:S(2)}) collective-permute-start(f32[5,4,8,512]{3,2,1,0:T(8,128)S(1)} %get-tuple-element.33), channel_id=1, source_target_pairs={{4,0},{8,4},{12,8},{16,12},{20,16},{24,20},{28,24},{5,1},{9,5},{13... | collective-permute-start | bytes 983048 | tf_op jit(solution)/shard_map/ppermute | solution.py:31
  245.1 71.4 %collective-permute-start.13 = (f32[32,8,1024]{2,1,0:T(8,128)S(1)}, f32[32,8,1024]{2,1,0:T(8,128)}, u32[]{:S(2)}, u32[]{:S(2)}) collective-permute-start(f32[32,8,1024]{2,1,0:T(8,128)S(1)} %constant_dynamic-update-slice_fusion.9), channel_id=1, source_target_pairs={{0,28},{2,30},{4,24},{6,26},{8,20},{10,22},{12,16},{14,18},{16,12}... | collective-permute-start | bytes 3145736 | tf_op jit(solution)/shard_map/ppermute | solution.py:155
  249.9 5.7 %copy-start.4 = (f32[1024,1024,1]{1,0,2:T(8,128)S(1)}, f32[1024,1024,1]{1,0,2:T(8,128)}, u32[]{:S(2)}) copy-start(f32[1024,1024,1]{1,0,2:T(8,128)} %constant.137) | copy-start | bytes 12582916
  249.9 5.7 %copy-start.13 = (f32[32,8,1024]{2,1,0:T(8,128)S(1)}, f32[32,8,1024]{2,1,0:T(8,128)}, u32[]{:S(2)}) copy-start(f32[32,8,1024]{2,1,0:T(8,128)} %copy-done.12) | copy-start | bytes 3145732
  255.7 3.3 copy-start.7
  255.7 3.3 copy-start.15
  265.5 54.0 %collective-permute-start.15 = (f32[32,8,1024]{2,1,0:T(8,128)}, f32[32,8,1024]{2,1,0:T(8,128)S(1)}, u32[]{:S(2)}, u32[]{:S(2)}) collective-permute-start(f32[32,8,1024]{2,1,0:T(8,128)} %constant_dynamic-update-slice_fusion.5), channel_id=1, source_target_pairs={{0,28},{2,30},{4,24},{6,26},{8,20},{10,22},{12,16},{14,18},{16,12}... | collective-permute-start | bytes 3145736 | tf_op jit(solution)/shard_map/ppermute | solution.py:155
  316.5 24.1 %collective-permute-start.17 = (f32[32,8,1024]{2,1,0:T(8,128)}, f32[32,8,1024]{2,1,0:T(8,128)}, u32[]{:S(2)}, u32[]{:S(2)}) collective-permute-start(f32[32,8,1024]{2,1,0:T(8,128)} %constant_dynamic-update-slice_fusion), channel_id=1, source_target_pairs={{0,28},{2,30},{4,24},{6,26},{8,20},{10,22},{12,16},{14,18},{16,12}... | collective-permute-start | bytes 3145736 | tf_op jit(solution)/shard_map/ppermute | solution.py:155
  326.4 5.7 %copy-start.8 = (f32[1024,1024,1]{1,0,2:T(8,128)S(1)}, f32[1024,1024,1]{1,0,2:T(8,128)}, u32[]{:S(2)}) copy-start(f32[1024,1024,1]{1,0,2:T(8,128)} %constant.136) | copy-start | bytes 12582916
  332.2 3.3 copy-start.5
  341.9 4.7 %copy-start.6 = (f32[1024,1024,1]{1,0,2:T(8,128)S(1)}, f32[1024,1024,1]{1,0,2:T(8,128)}, u32[]{:S(2)}) copy-start(f32[1024,1024,1]{1,0,2:T(8,128)} %constant.137) | copy-start | bytes 12582916
  346.7 3.8 copy-start.22
  346.7 3.8 copy-start.23
  346.7 3.8 copy-start.25
  346.7 3.8 copy-start.26
  346.7 3.8 copy-start.31
  346.7 3.8 copy-start.32
  350.5 2.2 copy-start.9
  351.8 3.0 copy-start.20
  351.8 3.0 copy-start.21
  351.9 3.0 copy-start.24
  351.9 3.0 copy-start.30
  354.9 2.2 copy-start.3
  359.5 24.5 %collective-permute-start.7 = (f32[32,8,512]{2,1,0:T(8,128)S(1)}, f32[32,8,512]{2,1,0:T(8,128)S(1)}, u32[]{:S(2)}, u32[]{:S(2)}) collective-permute-start(f32[32,8,512]{2,1,0:T(8,128)S(1)} %get-tuple-element.76), channel_id=1, source_target_pairs={{0,2},{2,0},{1,3},{3,1},{4,6},{6,4},{5,7},{7,5},{8,10},{10,8},{9,1... | collective-permute-start | bytes 1572872 | tf_op jit(solution)/shard_map/ppermute | solution.py:144
  365.7 20.0 %collective-permute-start.11 = (f32[32,8,512]{2,1,0:T(8,128)S(1)}, f32[32,8,512]{2,1,0:T(8,128)S(1)}, u32[]{:S(2)}, u32[]{:S(2)}) collective-permute-start(f32[32,8,512]{2,1,0:T(8,128)S(1)} %get-tuple-element.66), channel_id=1, source_target_pairs={{0,2},{2,0},{1,3},{3,1},{4,6},{6,4},{5,7},{7,5},{8,10},{10,8},{9,1... | collective-permute-start | bytes 1572872 | tf_op jit(solution)/shard_map/ppermute | solution.py:144
  371.1 25.9 %collective-permute-start.14 = (f32[32,8,512]{2,1,0:T(8,128)S(1)}, f32[32,8,512]{2,1,0:T(8,128)S(1)}, u32[]{:S(2)}, u32[]{:S(2)}) collective-permute-start(f32[32,8,512]{2,1,0:T(8,128)S(1)} %get-tuple-element.58), channel_id=1, source_target_pairs={{0,2},{2,0},{1,3},{3,1},{4,6},{6,4},{5,7},{7,5},{8,10},{10,8},{9,1... | collective-permute-start | bytes 1572872 | tf_op jit(solution)/shard_map/ppermute | solution.py:144
  377.2 31.0 %collective-permute-start.16 = (f32[32,8,512]{2,1,0:T(8,128)S(1)}, f32[32,8,512]{2,1,0:T(8,128)S(1)}, u32[]{:S(2)}, u32[]{:S(2)}) collective-permute-start(f32[32,8,512]{2,1,0:T(8,128)S(1)} %get-tuple-element.52), channel_id=1, source_target_pairs={{0,2},{2,0},{1,3},{3,1},{4,6},{6,4},{5,7},{7,5},{8,10},{10,8},{9,1... | collective-permute-start | bytes 1572872 | tf_op jit(solution)/shard_map/ppermute | solution.py:144
  380.0 17.0 %slice-start = ((s8[5242880]{0:T(1024)(128)(4,1)}), s8[4194304]{0:T(1024)(128)(4,1)S(1)}, s32[]{:S(2)}) async-start(s8[5242880]{0:T(1024)(128)(4,1)} %bitcast.215), calls=%async_computation | async-start | bytes 8388608
  380.0 17.0 %slice-start.1 = ((s8[5242880]{0:T(1024)(128)(4,1)}), s8[1048576]{0:T(1024)(128)(4,1)S(1)}, s32[]{:S(2)}) async-start(s8[5242880]{0:T(1024)(128)(4,1)} %bitcast.215), calls=%async_computation.1 | async-start | bytes 2097152
  382.5 32.8 %collective-permute-start.18 = (f32[32,8,512]{2,1,0:T(8,128)S(1)}, f32[32,8,512]{2,1,0:T(8,128)S(1)}, u32[]{:S(2)}, u32[]{:S(2)}) collective-permute-start(f32[32,8,512]{2,1,0:T(8,128)S(1)} %get-tuple-element.46), channel_id=1, source_target_pairs={{0,2},{2,0},{1,3},{3,1},{4,6},{6,4},{5,7},{7,5},{8,10},{10,8},{9,1... | collective-permute-start | bytes 1572872 | tf_op jit(solution)/shard_map/ppermute | solution.py:144
  408.2 7.3 %copy-start.2 = (f32[3,64,8,512]{3,2,1,0:T(8,128)S(1)}, f32[3,64,8,512]{3,2,1,0:T(8,128)}, u32[]{:S(2)}) copy-start(f32[3,64,8,512]{3,2,1,0:T(8,128)} %param.7) | copy-start | bytes 9437188
  408.2 7.3 %copy-start.27 = (f32[64,8,512]{2,1,0:T(8,128)S(1)}, f32[64,8,512]{2,1,0:T(8,128)}, u32[]{:S(2)}) copy-start(f32[64,8,512]{2,1,0:T(8,128)} %param.8) | copy-start | bytes 3145732
  408.2 7.3 %copy-start.28 = (f32[64,8,512]{2,1,0:T(8,128)S(1)}, f32[64,8,512]{2,1,0:T(8,128)}, u32[]{:S(2)}) copy-start(f32[64,8,512]{2,1,0:T(8,128)} %param.6) | copy-start | bytes 3145732
  415.5 4.1 copy-start.16

commit v2 on v1

v2 whole, which is shorter than its diff:
```python
import functools

import numpy as np
import jax
import jax.numpy as jnp
from jax import lax
from jax.experimental import pallas as pl
from jax.experimental.pallas import tpu as pltpu
from jax.sharding import PartitionSpec as P

HEAT_RATIO = 1.4
COURANT = 0.5
SECTION_DECAY = -5.0 / 9.0
SECTION_GAIN = 15.0 / 16.0
CUTOFF_BASE = 4.0
STENCIL = (0.8, -0.2, 4.0 / 105.0, -1.0 / 280.0)
FIELDS = 5
DEPTH = 2
MESH = pl.DeviceIdType.MESH


def trig_tables(half):
    points = np.arange(half)[:, None]
    tables = []
    for modes in (np.arange(0, half, 2), np.arange(1, half, 2)):
        phases = (points * modes[None, :] % (2 * half)) * (np.pi / half)
        tables.append(np.concatenate([np.cos(phases), np.sin(phases)], axis=1).astype(np.float32))
    table = np.stack(tables)
    high = table.astype(jnp.bfloat16)
    low = (table - high.astype(np.float32)).astype(jnp.bfloat16)
    return high, low


def split(values):
    high = values.astype(jnp.bfloat16)
    return high, (values - high.astype(jnp.float32)).astype(jnp.bfloat16)


def product(left_high, left_low, right_high, right_low, dims):
    dot = functools.partial(
        lax.dot_general, dimension_numbers=(dims, ((), ())), preferred_element_type=jnp.float32
    )
    return dot(left_high, right_high) + (dot(left_low, right_high) + dot(left_high, right_low))


def kernel(
    slabs, blocks, spacing,
    density, momentum, energy, trig, filt, table_high, table_low,
    out,
    g, rf, fz, fzr, ownx, other, az, xh, xl, yh, yl,
    zs, zr, ys, yr, rs, rr, hs, hr,
):
    rad, azi, ax = lax.axis_index("rad"), lax.axis_index("azi"), lax.axis_index("ax")
    rows, planes, angles = density.shape
    half = angles * blocks
    group = rows // blocks
    lines = group * planes
    mirror = slabs - 1 - rad
    upper = rad >= slabs // 2
    has_low, has_high = rad > 0, rad < slabs - 1

    def group_of(member):
        return jnp.where(upper, member, blocks - 1 - member) * group

    def peer(shift):
        return lax.rem(azi + shift, blocks)

    mine = group_of(azi)

    barrier = pltpu.get_barrier_semaphore()

    def greet(target):
        pl.semaphore_signal(barrier, inc=1, device_id=target, device_id_type=MESH)

    for shift in range(blocks):
        greet((mirror, peer(shift), ax))
        if shift:
            greet((rad, peer(shift), ax))
    greet((rad, azi, 1 - ax))

    @pl.when(has_low)
    def _():
        greet((rad - 1, azi, ax))

    @pl.when(has_high)
    def _():
        greet((rad + 1, azi, ax))

    def flux_row(l, _):
        rho, en = density[l], energy[l]
        mom = [momentum[c, l] for c in range(3)]
        inverse = 1.0 / rho
        vel = [m * inverse for m in mom]
        kinetic = mom[0] * vel[0] + mom[1] * vel[1] + mom[2] * vel[2]
        pressure = (HEAT_RATIO - 1.0) * (en - 0.5 * kinetic)
        radius = -1.0 + ((rad * rows + l).astype(jnp.float32) + 0.5) * spacing
        cosine, sine = trig[0], trig[1]
        scos, ssin = trig[2], trig[3]
        for f in range(FIELDS):
            parts = []
            for c in range(3):
                if f == 0:
                    value = mom[c]
                elif f == 4:
                    value = (en + pressure) * vel[c]
                else:
                    value = mom[f - 1] * vel[c]
                    if f - 1 == c:
                        value = value + pressure
                parts.append(value)
            g[f, l] = scos * parts[1] - ssin * parts[0]
            rf[f, l + 4] = radius * (cosine * parts[0] + sine * parts[1])
            fz[f, l] = parts[2]
        return 0

    lax.fori_loop(0, rows, flux_row, 0)

    pl.semaphore_wait(
        barrier, 2 * blocks + has_low.astype(jnp.int32) + has_high.astype(jnp.int32)
    )

    def remote(source, target, send, recv, device):
        return pltpu.make_async_remote_copy(
            src_ref=source, dst_ref=target, send_sem=send, recv_sem=recv,
            device_id=device, device_id_type=MESH,
        )

    to_high = remote(
        rf.at[:, pl.ds(rows, 4)], rf.at[:, pl.ds(0, 4)], hs.at[0], hr.at[0],
        (jnp.minimum(rad + 1, slabs - 1), azi, ax),
    )
    to_low = remote(
        rf.at[:, pl.ds(4, 4)], rf.at[:, pl.ds(rows + 4, 4)], hs.at[1], hr.at[1],
        (jnp.maximum(rad - 1, 0), azi, ax),
    )
    across = remote(fz, fzr, hs.at[2], hr.at[2], (rad, azi, 1 - ax))

    def z_copy(f, member, slot):
        return remote(
            g.at[f, pl.ds(group_of(member), group)], other.at[f, slot],
            zs.at[f, member], zr.at[f, slot], (mirror, member, ax),
        )

    def y_copy(f, member, slot):
        return remote(
            g.at[f, pl.ds(group_of(member), group)], ownx.at[f, slot],
            ys.at[f, member], yr.at[f, slot], (rad, member, ax),
        )

    def r_copy(f, member, source):
        return remote(
            g.at[f, pl.ds(member * group, group)], az.at[f, pl.ds(group_of(source), group)],
            rs.at[f, member], rr.at[f, source], (rad, member, ax),
        )

    def launch(f):
        for shift in range(blocks):
            z_copy(f, peer(shift), azi).start()
        for shift in range(1, blocks):
            y_copy(f, peer(shift), azi).start()

    @pl.when(has_high)
    def _():
        to_high.start()

    @pl.when(has_low)
    def _():
        to_low.start()

    for f in range(DEPTH):
        launch(f)
    across.start()

    @pl.when(jnp.logical_not(has_low))
    def _():
        rf[:, pl.ds(0, 4)] = jnp.zeros((FIELDS, 4, planes, angles), jnp.float32)

    @pl.when(jnp.logical_not(has_high))
    def _():
        rf[:, pl.ds(rows + 4, 4)] = jnp.zeros((FIELDS, 4, planes, angles), jnp.float32)

    @pl.when(has_low)
    def _():
        to_high.wait_recv()
        to_low.wait_send()

    @pl.when(has_high)
    def _():
        to_low.wait_recv()
        to_high.wait_send()

    across.wait()
    is_first = jnp.where(ax == 0, 1.0, 0.0).astype(jnp.float32)
    plane_ids = lax.broadcasted_iota(jnp.int32, (planes, angles), 0)

    def local_row(l, _):
        radius = -1.0 + ((rad * rows + l).astype(jnp.float32) + 0.5) * spacing
        scale = 1.0 / (jnp.full((planes, angles), spacing, jnp.float32) * radius)
        for f in range(FIELDS):
            radial = 0.0
            axial = 0.0
            own, far = fz[f, l], fzr[f, l]
            high, low = far * is_first, far * (1.0 - is_first)
            for m, weight in enumerate(STENCIL, start=1):
                radial = radial + weight * (rf[f, l + 4 + m] - rf[f, l + 4 - m])
                ahead = pltpu.roll(jnp.where(plane_ids < m, high, own), planes - m, 0)
                behind = pltpu.roll(jnp.where(plane_ids >= planes - m, low, own), m, 0)
                axial = axial + weight * (ahead - behind)
            out[f, l] = radial * scale + axial * (1.0 / spacing)
        return 0

    lax.fori_loop(0, rows, local_row, 0)

    tile = min(256, half)
    point_tile = min(256, angles)
    quarters = half // tile

    def add_in(f):
        for shift in range(1, blocks):
            source = peer(shift)
            r_copy(f, source, source).wait_recv()

        def add_row(l, _):
            out[f, l] = out[f, l] + az[f, l]
            return 0

        lax.fori_loop(0, rows, add_row, 0)

    def step(f, _):
        for shift in range(blocks):
            z_copy(f, peer(shift), peer(shift)).wait_recv()
        for shift in range(1, blocks):
            y_copy(f, peer(shift), peer(shift)).wait_recv()

        @pl.when(f + DEPTH < FIELDS)
        def _():
            launch(f + DEPTH)

        for shift in range(blocks):
            z_copy(f, peer(shift), azi).wait_send()
        for shift in range(1, blocks):
            y_copy(f, peer(shift), azi).wait_send()

        def copy_own(i, _):
            ownx[f, azi, i] = g[f, mine + i]
            return 0

        lax.fori_loop(0, group, copy_own, 0)

        def mix(i, _):
            j, k = i // (group // 2), lax.rem(i, group // 2)
            near = jnp.concatenate([ownx[f, j, 2 * k], ownx[f, j, 2 * k + 1]], axis=0)
            back = group - 1 - 2 * k
            far = jnp.concatenate([other[f, j, back], other[f, j, back - 1]], axis=0)
            place = pl.ds(pl.multiple_of(k * 2 * planes, 2 * planes), 2 * planes)
            for par, value in enumerate((near + far, near - far)):
                top, rest = split(value)
                xh[par, j, place] = top
                xl[par, j, place] = rest
            return 0

        lax.fori_loop(0, blocks * group // 2, mix, 0)

        def forward(i, _):
            par, t = i // quarters, lax.rem(i, quarters)
            columns = pl.ds(pl.multiple_of(t * tile, tile), tile)
            total = jnp.zeros((lines, tile), jnp.float32)
            for j in range(blocks):
                total = total + product(
                    xh[par, j], xl[par, j],
                    table_high[par, j, :, columns], table_low[par, j, :, columns], ((1,), (0,)),
                )
            scaled = total * filt[par, :, columns]
            moved = lax.rem(t + quarters // 2, quarters)
            target = pl.ds(pl.multiple_of(moved * tile, tile), tile)
            top, rest = split(scaled)
            yh[par, :, target] = top
            yl[par, :, target] = rest
            return 0

        lax.fori_loop(0, 2 * quarters, forward, 0)

        def inverse(i, _):
            per = angles // point_tile
            j, p = i // per, lax.rem(i, per)
            points = pl.ds(pl.multiple_of(p * point_tile, point_tile), point_tile)
            total = 0.0
            for par in range(2):
                total = total + product(
                    yh[par], yl[par], table_high[par, j, points, :], table_low[par, j, points, :],
                    ((1,), (1,)),
                )
            g[f, pl.ds(j * group, group), :, points] = total.reshape(group, planes, point_tile)
            return 0

        lax.fori_loop(0, blocks * (angles // point_tile), inverse, 0)

        for shift in range(1, blocks):
            r_copy(f, peer(shift), azi).start()

        def keep_own(i, _):
            az[f, mine + i] = g[f, azi * group + i]
            return 0

        lax.fori_loop(0, group, keep_own, 0)

        @pl.when(f >= 1)
        def _():
            add_in(f - 1)

        return 0

    lax.fori_loop(0, FIELDS, step, 0)
    add_in(FIELDS - 1)
    for f in range(FIELDS):
        for shift in range(1, blocks):
            r_copy(f, peer(shift), azi).wait_send()


def per_device(density, momentum, energy, register):
    slabs = lax.axis_size("rad")
    blocks = lax.axis_size("azi")
    rad_index = lax.axis_index("rad")
    azi_index = lax.axis_index("azi")
    rows, planes, angles = density.shape
    half = angles * blocks
    spacing = 2.0 / (rows * slabs)
    group = rows // blocks
    lines = group * planes
    upper = rad_index >= slabs // 2

    azimuths = jnp.pi * (azi_index * angles + jnp.arange(angles)).astype(jnp.float32) / half
    cosine, sine = jnp.cos(azimuths), jnp.sin(azimuths)
    sign = jnp.where(upper, 1.0, -1.0).astype(jnp.float32)
    trig = jnp.broadcast_to(
        jnp.stack([cosine, sine, sign * cosine, sign * sine])[:, None, :], (4, planes, angles)
    )
    mine = jnp.where(upper, azi_index, blocks - 1 - azi_index) * group
    row_ids = rad_index * rows + mine + jnp.arange(group)
    distance = jnp.abs(-1.0 + (row_ids.astype(jnp.float32) + 0.5) * spacing)[None, :, None]
    modes = jnp.stack([jnp.arange(0, half, 2), jnp.arange(1, half, 2)]).astype(jnp.float32)[:, None]
    weight = modes / half / (1.0 + (modes / (CUTOFF_BASE + half * distance)) ** 8) / distance
    weight = jnp.concatenate([-weight, weight], axis=-1)
    filt = jnp.broadcast_to(weight[:, :, None, :], (2, group, planes, half)).reshape(2, lines, half)
    high, low = trig_tables(half)
    high = high.reshape(2, blocks, angles, half)
    low = low.reshape(2, blocks, angles, half)

    f32, bf16 = jnp.float32, jnp.bfloat16
    vmem, dma = pltpu.VMEM, pltpu.SemaphoreType.DMA
    block = (FIELDS, rows, planes, angles)
    pieces = (FIELDS, blocks, group, planes, angles)
    term = pl.pallas_call(
        functools.partial(kernel, slabs, blocks, spacing),
        out_shape=jax.ShapeDtypeStruct(block, f32),
        in_specs=[pl.BlockSpec(memory_space=pltpu.VMEM)] * 7,
        out_specs=pl.BlockSpec(memory_space=pltpu.VMEM),
        scratch_shapes=[
            vmem(block, f32),
            vmem((FIELDS, rows + 8, planes, angles), f32),
            vmem(block, f32),
            vmem(block, f32),
            vmem(pieces, f32),
            vmem(pieces, f32),
            vmem(block, f32),
            vmem((2, blocks, lines, angles), bf16),
            vmem((2, blocks, lines, angles), bf16),
            vmem((2, lines, half), bf16),
            vmem((2, lines, half), bf16),
        ] + [dma((FIELDS, blocks))] * 6 + [dma((3,))] * 2,
        compiler_params=pltpu.CompilerParams(
            collective_id=0, has_side_effects=True, vmem_limit_bytes=63 * 2**20
        ),
    )(density, momentum, energy, trig, filt, jnp.asarray(high), jnp.asarray(low))
    conserved = jnp.concatenate([density[None], momentum, energy[None]], axis=0)
    register_new = SECTION_DECAY * register - COURANT * spacing * term
    state_new = conserved + SECTION_GAIN * register_new
    return (register_new, state_new)


def solution(mesh):
    placed = (
        P("rad", "ax", "azi"),
        P(None, "rad", "ax", "azi"),
        P("rad", "ax", "azi"),
        P(None, "rad", "ax", "azi"),
    )
    return jax.shard_map(
        per_device,
        mesh=mesh,
        in_specs=placed,
        out_specs=(P(None, "rad", "ax", "azi"), P(None, "rad", "ax", "azi")),
        check_vma=False,
    )
```

time: 428 us -> 305 us (0.71)
  the two profiles are of different devices: /device:TPU:8 before, /device:TPU:20 now
where the time goes in v2:
time: 305 us; the launch traced here: 304 us
  Pallas kernels  292 us (96%)
  other arithmetic  9.65 us (3%)
    pallas_call x1, Pallas kernels, per_device(): pl.pallas_call(functools.partial(kernel, slabs, blocks, spacing), out_sha...  292 us
    add x1, other arithmetic, per_device(): state_new = conserved + SECTION_GAIN * register_new  9.29 us

profile of v2, /device:TPU:20, one launch (start us, length us, event | category | flops | bytes accessed | tf_op | source)
XLA Modules:
  0.0 304.5 jit_solution(7969586469861505633)
XLA Ops:
  0.7 0.1 broadcast_multiply_fusion.1
  0.7 0.1 fusion.6
  0.9 0.6 broadcast_in_dim.8.trig
  1.5 0.1 fusion.5
  1.7 1.6 broadcast_bitcast_fusion.filt
  3.3 291.9 %shard_map.77 = f32[5,64,8,512]{3,2,1,0:T(8,128)} custom-call(f32[64,8,512]{2,1,0:T(8,128)} %density.1, f32[3,64,8,512]{3,2,1,0:T(8,128)} %momentum.1, f32[64,8,512]{2,1,0:T(8,128)} %energy.1, f32[4,8,512]{2,1,0:T(8,128)} %broadcast_in_dim.8.trig, f32[2,256,1024]{2,1,0:T(8,128)} %broadcast_bitcast_fusion.filt, ...), custom_call_target="tpu_custom_call" | custom-call | tf_op jit(solution)/shard_map/pallas_call | solution.py:353
  295.2 9.3 %maximum_add_fusion = (f32[5,64,8,512]{3,2,1,0:T(8,128)}, f32[5,64,8,512]{3,2,1,0:T(8,128)}) fusion(f32[1,64,8,512]{3,2,1,0:T(8,128)} %bitcast.4, f32[3,64,8,512]{3,2,1,0:T(8,128)} %momentum.1, f32[1,64,8,512]{3,2,1,0:T(8,128)} %bitcast.5, f32[5,64,8,512]{3,2,1,0:T(8,128)} %shard_map.77, f32[5,64,8,512]{3,2,1,0:T(8,128)} %param.9), kind=kLoop, calls=%fused_computation | loop fusion | flops 9175040 | bytes 26214400 | tf_op jit(solution)/shard_map/add | solution.py:377
  (6 shorter events, 0.1 us)

commit v3 on v2

--- a/solution.py
+++ b/solution.py
@@ -15,7 +15,7 @@
 CUTOFF_BASE = 4.0
 STENCIL = (0.8, -0.2, 4.0 / 105.0, -1.0 / 280.0)
 FIELDS = 5
-DEPTH = 2
+EARLY = 2
 MESH = pl.DeviceIdType.MESH
 
 
@@ -135,10 +135,16 @@
     )
     across = remote(fz, fzr, hs.at[2], hr.at[2], (rad, azi, 1 - ax))
 
-    def z_copy(f, member, slot):
+    def z_copy(f):
         return remote(
-            g.at[f, pl.ds(group_of(member), group)], other.at[f, slot],
-            zs.at[f, member], zr.at[f, slot], (mirror, member, ax),
+            g.at[f, pl.ds(mine, group)], other.at[f, azi],
+            zs.at[f, azi], zr.at[f, azi], (mirror, azi, ax),
+        )
+
+    def forward_copy(f, member):
+        return remote(
+            ownx.at[f, member], other.at[f, member],
+            zs.at[f, member], zr.at[f, member], (mirror, azi, ax),
         )
 
     def y_copy(f, member, slot):
@@ -154,10 +160,14 @@
         )
 
     def launch(f):
-        for shift in range(blocks):
-            z_copy(f, peer(shift), azi).start()
         for shift in range(1, blocks):
             y_copy(f, peer(shift), azi).start()
+        z_copy(f).start()
+
+    def pass_on(f):
+        for shift in range(1, blocks):
+            y_copy(f, peer(shift), peer(shift)).wait_recv()
+            forward_copy(f, peer(shift)).start()
 
     @pl.when(has_high)
     def _():
@@ -167,9 +177,11 @@
     def _():
         to_low.start()
 
-    for f in range(DEPTH):
+    for f in range(FIELDS):
         launch(f)
     across.start()
+    for f in range(EARLY):
+        pass_on(f)
 
     @pl.when(jnp.logical_not(has_low))
     def _():
@@ -210,6 +222,8 @@
         return 0
 
     lax.fori_loop(0, rows, local_row, 0)
+    for f in range(EARLY, FIELDS):
+        pass_on(f)
 
     tile = min(256, half)
     point_tile = min(256, angles)
@@ -227,18 +241,9 @@
         lax.fori_loop(0, rows, add_row, 0)
 
     def step(f, _):
-        for shift in range(blocks):
-            z_copy(f, peer(shift), peer(shift)).wait_recv()
-        for shift in range(1, blocks):
-            y_copy(f, peer(shift), peer(shift)).wait_recv()
-
-        @pl.when(f + DEPTH < FIELDS)
-        def _():
-            launch(f + DEPTH)
-
-        for shift in range(blocks):
-            z_copy(f, peer(shift), azi).wait_send()
-        for shift in range(1, blocks):
+        z_copy(f).wait()
+        for shift in range(1, blocks):
+            forward_copy(f, peer(shift)).wait()
             y_copy(f, peer(shift), azi).wait_send()
 
         def copy_own(i, _):
@@ -280,9 +285,10 @@
 
         lax.fori_loop(0, 2 * quarters, forward, 0)
 
+        per = angles // point_tile
+
         def inverse(i, _):
-            per = angles // point_tile
-            j, p = i // per, lax.rem(i, per)
+            j, p = lax.rem(azi + 1 + i // per, blocks), lax.rem(i, per)
             points = pl.ds(pl.multiple_of(p * point_tile, point_tile), point_tile)
             total = 0.0
             for par in range(2):
@@ -293,10 +299,10 @@
             g[f, pl.ds(j * group, group), :, points] = total.reshape(group, planes, point_tile)
             return 0
 
-        lax.fori_loop(0, blocks * (angles // point_tile), inverse, 0)
-
+        lax.fori_loop(0, (blocks - 1) * per, inverse, 0)
         for shift in range(1, blocks):
             r_copy(f, peer(shift), azi).start()
+        lax.fori_loop((blocks - 1) * per, blocks * per, inverse, 0)
 
         def keep_own(i, _):
             az[f, mine + i] = g[f, azi * group + i]

time: 305 us -> 279 us (0.915)
  Pallas kernels: 292 us -> 265 us
    pallas_call x1, Pallas kernels: 292 us -> 265 us  [per_device(): pl.pallas_call(functools.partial(kernel, slabs, blocks, spacing), out_sha...]
where the time goes in v3:
time: 279 us; the launch traced here: 278 us
  Pallas kernels  265 us (95%)
  other arithmetic  9.65 us (3%)
    pallas_call x1, Pallas kernels, per_device(): pl.pallas_call(functools.partial(kernel, slabs, blocks, spacing), out_sha...  265 us
    add x1, other arithmetic, per_device(): state_new = conserved + SECTION_GAIN * register_new  9.29 us

profile of v3, /device:TPU:20, one launch (start us, length us, event | category | flops | bytes accessed | tf_op | source)
XLA Modules:
  0.0 277.7 jit_solution(990171449578110947)
XLA Ops:
  0.7 0.1 broadcast_multiply_fusion.1
  0.7 0.1 fusion.6
  0.9 0.6 broadcast_in_dim.8.trig
  1.5 0.1 fusion.5
  1.7 1.6 broadcast_bitcast_fusion.filt
  3.3 265.2 %shard_map.77 = f32[5,64,8,512]{3,2,1,0:T(8,128)} custom-call(f32[64,8,512]{2,1,0:T(8,128)} %density.1, f32[3,64,8,512]{3,2,1,0:T(8,128)} %momentum.1, f32[64,8,512]{2,1,0:T(8,128)} %energy.1, f32[4,8,512]{2,1,0:T(8,128)} %broadcast_in_dim.8.trig, f32[2,256,1024]{2,1,0:T(8,128)} %broadcast_bitcast_fusion.filt, ...), custom_call_target="tpu_custom_call" | custom-call | tf_op jit(solution)/shard_map/pallas_call | solution.py:359
  268.5 9.3 %maximum_add_fusion = (f32[5,64,8,512]{3,2,1,0:T(8,128)}, f32[5,64,8,512]{3,2,1,0:T(8,128)}) fusion(f32[1,64,8,512]{3,2,1,0:T(8,128)} %bitcast.4, f32[3,64,8,512]{3,2,1,0:T(8,128)} %momentum.1, f32[1,64,8,512]{3,2,1,0:T(8,128)} %bitcast.5, f32[5,64,8,512]{3,2,1,0:T(8,128)} %shard_map.77, f32[5,64,8,512]{3,2,1,0:T(8,128)} %param.9), kind=kLoop, calls=%fused_computation | loop fusion | flops 9175040 | bytes 26214400 | tf_op jit(solution)/shard_map/add | solution.py:383
  (6 shorter events, 0.1 us)
